TPU v7x, 32 devices: a whole 2x2x4 slice. The times are simulated.
32 devices in a mesh: gy: 16 (over z, y, core), var: 2 (over x).
Axes of the slice: x: 2, y: 2, z: 4, core: 2. Of those that a mesh axis runs over, the one named last changes fastest.
Arguments:
- field: float32 [32, 32, 512, 128], P('var', None, 'gy')
- factor_x: float32 [32, 16], replicated, may hold values from -1 to 1
- factor_y: float32 [512, 64], P('gy'), may hold values from -0.25 to 0.25
- factor_z: float32 [128, 64], replicated, may hold values from -0.5 to 0.5
- factor_v: float32 [32, 16], replicated, may hold values from -1 to 1
Outputs:
- proj_z: float32 [128, 128], replicated
- proj_v: float32 [32, 32], replicated
- core_rms: float32 [], replicated
All inputs are finite; a program needn't handle non-finite values.
Results may differ from a plain program's by a relative error of at most 0.0003.
Values sent between devices are 32-bit elements; how exact they have to be, the bound alone decides.
A program may use at most 192 MiB of HBM per device.

v0:
```python
import jax
import jax.numpy as jnp
from jax import lax
from jax.sharding import PartitionSpec as P

precise = lax.Precision.HIGHEST


def orth(mat):
    gram = jnp.dot(mat.T, mat, precision=precise)
    lower = jnp.linalg.cholesky(gram)
    return jax.scipy.linalg.solve_triangular(lower, mat.T, lower=True).T


def total_core(local_part):
    return lax.psum(local_part, ("gy", "var"))


def per_device(field, factor_x, factor_y, factor_z, factor_v):
    var_rows = field.shape[0]
    var_start = lax.axis_index("var") * var_rows
    local_v = lax.dynamic_slice_in_dim(factor_v, var_start, var_rows, 0)
    along_x = jnp.einsum("vxyz,xa->vayz", field, factor_x, precision=precise)
    partial_value = jnp.einsum("vayz,yb->vabz", along_x, factor_y, precision=precise)
    wide_z = jnp.einsum("vabz,vc->cabz", partial_value, local_v, precision=precise)
    fibres = lax.psum_scatter(wide_z, ("gy", "var"), scatter_dimension=3, tiled=True)
    z_count = fibres.shape[3]
    z_start = lax.axis_index(("gy", "var")) * z_count
    local_z = lax.dynamic_slice_in_dim(factor_z, z_start, z_count, 0)
    small_core = total_core(jnp.einsum("cabz,zr->cabr", fibres, local_z, precision=precise))
    rows_z = jnp.einsum("cabz,cabr->zr", fibres, small_core, precision=precise)
    raw_z = lax.all_gather(rows_z, ("gy", "var"), axis=0, tiled=True)
    new_z = orth(raw_z)
    proj_z = jnp.dot(new_z, new_z.T, precision=precise)
    wide_v = jnp.einsum("vabz,zr->vabr", partial_value, new_z, precision=precise)
    flat_v = wide_v.reshape(var_rows, -1)
    summed_v = lax.psum(flat_v, "gy")
    every_v = lax.all_gather(summed_v, "var", axis=0, tiled=True)
    gram_v = jnp.dot(every_v, every_v.T, precision=precise)
    new_v = orth(jnp.dot(gram_v, factor_v, precision=precise))
    proj_v = jnp.dot(new_v, new_v.T, precision=precise)
    core = jnp.dot(new_v.T, every_v, precision=precise)
    core_rms = jnp.sqrt(jnp.mean(core * core))
    return (proj_z, proj_v, core_rms)


def solution(mesh):
    in_specs = (P("var", None, "gy", None), P(), P("gy", None), P(), P())
    out_specs = (P(), P(), P())
    return jax.shard_map(
        per_device, mesh=mesh, in_specs=in_specs, out_specs=out_specs, check_vma=False
    )
```

profile of v0, /device:TPU:0, one launch (start us, length us, event | category | flops | bytes accessed | tf_op | source)
XLA Modules:
  0.0 1088.3 jit_solution(6154609231923412082)
XLA Ops:
  7.2 12.7 %fusion = f32[16,16,32,128]{3,0,2,1:T(8,128)S(1)} fusion(f32[16,32,32,128]{3,2,1,0:T(8,128)} %param.5, f32[32,16]{0,1:T(8,128)} %param.6), kind=kOutput, calls=%fused_computation.1 | convolution fusion | flops 402653184 | bytes 12584960 | tf_op jit(solution)/shard_map/vxyz,xa->vayz/dot_general | solution.py:23
  20.0 8.3 fusion.7
  28.3 3.2 copy-done.1
  31.5 109.4 %fusion.2 = f32[16,16,64,128]{0,3,2,1:T(8,128)} fusion(f32[16,16,64,128]{3,2,1,0:T(8,128)S(1)} %fusion.7, f32[32,16]{0,1:T(8,128)S(1)} %copy-done.3, s32[]{:T(128)S(6)} %select_n.14), kind=kOutput, calls=%fused_computation.3 | convolution fusion | flops 402653184 | bytes 16779268 | tf_op jit(solution)/shard_map/vabz,vc->cabz/dot_general | solution.py:25
  140.9 42.7 %copy.15 = f32[16,16,64,128]{2,1,0,3:T(8,128)} copy(f32[16,16,64,128]{0,3,2,1:T(8,128)} %fusion.2) | data formatting | bytes 16777216 | tf_op jit(solution)/shard_map/vabz,vc->cabz/dot_general | solution.py:25
  183.6 360.1 %reduce-scatter.2.cloned.1.call-done = f32[16,16,64,4]{2,1,0,3:T(8,128)} async-done(((f32[16,16,64,128]{2,1,0,3:T(8,128)}), f32[16,16,64,4]{2,1,0,3:T(8,128)}) %reduce-scatter.2.cloned.1.call-update) | async-done | bytes 262160 | tf_op jit(solution)/shard_map/reduce_scatter | solution.py:26
  543.8 16.5 %fusion.11 = f32[16,16,64,64]{3,2,0,1:T(8,128)} fusion(f32[16,16,64,4]{2,1,0,3:T(8,128)} %reduce-scatter.2.cloned.1.call-done, f32[128,64]{0,1:T(8,128)S(1)} %copy-done, s32[]{:T(128)S(6)} %select_n.15), kind=kOutput, calls=%fused_computation.11 | convolution fusion | flops 50331648 | bytes 4489220 | tf_op jit(solution)/shard_map/cabz,zr->cabr/dot_general | solution.py:30
  560.3 179.9 %all-reduce.3.cloned.1.call-done = f32[16,16,64,64]{3,2,0,1:T(8,128)} async-done(((f32[16,16,64,64]{3,2,0,1:T(8,128)}), f32[16,16,64,64]{3,2,0,1:T(8,128)}) %all-reduce.3.cloned.1.call-update) | async-done | bytes 4194320 | tf_op jit(solution)/shard_map/psum | solution.py:16
  740.2 6.8 convolution_bitcast_fusion
  747.0 67.6 %all-gather = f32[32,4,64]{2,1,0:T(4,128)S(1)} all-gather(f32[1,4,64]{2,1,0:T(4,128)S(1)} %convolution_bitcast_fusion), channel_id=1, replica_groups=mesh['gy'=16,'var'=2] {'gy','var'}, dimensions={0}, use_global_device_ids=true | all-gather | bytes 33792 | tf_op jit(solution)/shard_map/all_gather | solution.py:32
  814.6 0.3 fusion.32
  814.9 0.1 copy.17
  815.0 5.8 cholesky.29
  820.9 0.6 compare_reduce_fusion.1
  821.5 0.7 fusion.14
  822.2 4.9 custom-call.14
  827.1 0.3 fusion.17
  827.4 10.9 %fusion.15 = f32[16,16,64,64]{3,2,1,0:T(8,128)} fusion(f32[16,16,64,128]{3,2,1,0:T(8,128)} %copy-done.1, f32[64,128]{1,0:T(8,128)S(1)} %fusion.17), kind=kOutput, calls=%fused_computation.16 | convolution fusion | flops 1610612736 | bytes 12615680 | tf_op jit(solution)/shard_map/vabz,zr->vabr/dot_general | solution.py:35
  838.3 6.0 reshape.28
  844.4 107.5 %all-reduce.5.cloned.1.call-done = f32[16,65536]{1,0:T(8,128)} async-done(((f32[16,65536]{1,0:T(8,128)}), f32[16,65536]{1,0:T(8,128)}) %all-reduce.5.cloned.1.call-update) | async-done | bytes 4194320 | tf_op jit(solution)/shard_map/psum | solution.py:37
  951.9 0.9 fusion.33
  952.8 103.5 %all-gather.3.cloned.1.call-done = f32[32,65536]{1,0:T(8,128)} async-done(((f32[16,65536]{1,0:T(8,128)}), f32[32,65536]{1,0:T(8,128)}) %all-gather.3.cloned.1.call-update) | async-done | bytes 8388624 | tf_op jit(solution)/shard_map/all_gather | solution.py:38
  1056.3 10.4 fusion.34
  1066.7 0.1 fusion.35
  1066.9 0.1 fusion.36
  1067.1 1.5 cholesky.61
  1068.6 0.6 compare_reduce_fusion
  1069.2 0.6 fusion.23
  1069.9 1.2 custom-call.15
  1071.1 0.2 fusion.26
  1071.3 0.8 fusion.37
  1072.2 7.5 fusion.10
  (22 shorter events, 0.4 us)
Async XLA Ops:
  7.2 536.6 %copy-start = (f32[128,64]{0,1:T(8,128)S(1)}, f32[128,64]{0,1:T(8,128)}, u32[]{:S(2)}) copy-start(f32[128,64]{0,1:T(8,128)} %param.8) | copy-start | bytes 98308
  7.2 12.8 %copy-start.4 = (f32[32,64]{1,0:T(8,128)S(1)}, f32[32,64]{1,0:T(8,128)}, u32[]{:S(2)}) copy-start(f32[32,64]{1,0:T(8,128)} %param.7) | copy-start | bytes 24580
  7.2 536.6 %reduce-scatter.2.cloned.1.call-start = ((), (), s32[]{:S(2)}) async-start(), calls=%async_computation.1 | async-start | bytes 17301504 | tf_op jit(solution)/shard_map/reduce_scatter | solution.py:26
  20.0 11.5 %copy-start.3 = (f32[32,16]{0,1:T(8,128)S(1)}, f32[32,16]{0,1:T(8,128)}, u32[]{:S(2)}) copy-start(f32[32,16]{0,1:T(8,128)} %param.9) | copy-start | bytes 6148
  28.3 3.2 copy-start.1
  183.6 556.6 %all-reduce.3.cloned.1.call-start = ((), (), s32[]{:S(2)}) async-start(), calls=%async_computation.2 | async-start | bytes 16777216 | tf_op jit(solution)/shard_map/psum | solution.py:16
  543.8 196.4 %copy-start.2 = (f32[16,16,64,4]{2,1,0,3:T(8,128)S(1)}, f32[16,16,64,4]{2,1,0,3:T(8,128)}, u32[]{:S(2)}) copy-start(f32[16,16,64,4]{2,1,0,3:T(8,128)} %reduce-scatter.2.cloned.1.call-done) | copy-start | bytes 786436
  560.2 391.6 %all-reduce.5.cloned.1.call-start = ((), (), s32[]{:S(2)}) async-start(), calls=%async_computation.3 | async-start | bytes 8388608 | tf_op jit(solution)/shard_map/psum | solution.py:37
  844.3 212.0 %all-gather.3.cloned.1.call-start = ((), (), s32[]{:S(2)}) async-start(), calls=%async_computation.4 | async-start | bytes 12582912 | tf_op jit(solution)/shard_map/all_gather | solution.py:38
Sparse Core Ops, SparseCore 0:
  183.7 360.0 reduce-scatter.1
  560.4 179.7 all-reduce.2
  844.4 107.3 all-reduce.4
  953.3 102.9 all-gather.2
where the time goes:
time: 1090 us
  waiting for transfers between devices  751 us (69%)
  matrix products  185 us (17%)
  blocking collectives  67.6 us (6%)
  local copies, waits for them, and re-layouts  52 us (5%)
  other arithmetic  16.1 us (1%)
  between operations  16 us (1%)
    reduce_scatter x1, waiting for transfers between devices, per_device(): lax.psum_scatter(wide_z, ('gy', 'var'), scatter_dimension=3, tiled=True)  360 us
    psum x1, waiting for transfers between devices, total_core(): return lax.psum(local_part, ('gy', 'var'))  180 us
    dot_general x1, matrix products, per_device(): jnp.einsum('vabz,vc->cabz', partial_value, local_v, precision=precise)  109 us
    psum x1, waiting for transfers between devices, per_device(): summed_v = lax.psum(flat_v, 'gy')  108 us
    all_gather x1, waiting for transfers between devices, per_device(): every_v = lax.all_gather(summed_v, 'var', axis=0, tiled=True)  103 us
    all_gather x1, blocking collectives, per_device(): raw_z = lax.all_gather(rows_z, ('gy', 'var'), axis=0, tiled=True)  67.6 us
    dot_general x1, local copies, waits for them, and re-layouts, per_device(): jnp.einsum('vabz,vc->cabz', partial_value, local_v, precision=precise)  42.7 us
  transfers between devices with their start and end apart: 4, of which 4 were waited for; matrix products, arithmetic and copies ran while one was open for 0% of the time, Pallas kernels for 0%

commit v1 on v0

v1 whole, which is shorter than its diff:
```python
import functools

import jax
import jax.numpy as jnp
from jax import lax
from jax.experimental import pallas as pl
from jax.experimental.pallas import tpu as pltpu
from jax.sharding import PartitionSpec as P

MESH = pl.DeviceIdType.MESH
F32 = jnp.float32
BF16 = jnp.bfloat16
N_CORE = 2
N_Z = 4


def exact(a, b, ca=1, cb=0):
    return lax.dot_general(
        a, b, (((ca,), (cb,)), ((), ())),
        precision=lax.Precision.HIGHEST, preferred_element_type=F32,
    )


def split(a):
    high = a.astype(BF16)
    return high, (a - high.astype(F32)).astype(BF16)


def three(a, b):
    def dot(p, q):
        return lax.dot_general(p, q, (((1,), (0,)), ((), ())), preferred_element_type=F32)
    return dot(a[0], b[0]) + (dot(a[0], b[1]) + dot(a[1], b[0]))


def iota(shape, dim):
    return lax.broadcasted_iota(jnp.int32, shape, dim)


def spread(shape, row_div, row_mod, col_div, col_mod):
    rows = (iota(shape, 0) // row_div) % row_mod
    cols = (iota(shape, 1) // col_div) % col_mod
    return (rows == cols).astype(F32)


def kron_eye(factor, eye):
    k, m = factor.shape
    tall = exact(spread((m * eye, m), eye, m, 1, m), factor, 1, 1)
    full = exact(tall, spread((k, k * eye), 1, k, eye, k))
    return full * spread((m * eye, k * eye), 1, eye, 1, eye)


def eye_kron(factor, eye):
    k, m = factor.shape
    tall = exact(spread((m * eye, m), 1, m, 1, m), factor, 1, 1)
    full = exact(tall, spread((k, k * eye), 1, k, 1, k))
    return full * spread((m * eye, k * eye), m, eye, k, eye)


def orth_rows(mat_t):
    rank = mat_t.shape[0]
    gram = exact(mat_t, mat_t, 1, 1)
    left = [gram[g:g + 8] for g in range(0, rank, 8)]
    right = [mat_t[g:g + 8] for g in range(0, rank, 8)]
    done = []
    for i in range(rank):
        g, k = i // 8, i % 8
        row_l, row_r = left[g][k:k + 1], right[g][k:k + 1]
        pivot = row_l[:, i:i + 1]
        inverse = 1.0 / pivot
        scaled_l, scaled_r = row_l * inverse, row_r * inverse
        done.append(row_r * lax.rsqrt(pivot))
        for h in range(g, rank // 8):
            col = left[h][:, i:i + 1]
            if h == g:
                col = jnp.where(iota((8, 1), 0) > k, col, 0.0)
            left[h] = left[h] - col * scaled_l
            right[h] = right[h] - col * scaled_r
    return jnp.concatenate(done, axis=0)


def kernel(
    n_y, n_var, core_size,
    field, fx_ref, fy_ref, fz_ref, fv_ref,
    proj_z_ref, proj_v_ref, rms_ref,
    fbuf, ax, axr, fy_own, fy_sib, acc,
    y_right, y_left, z_right, z_left, pown,
    red_z, red_v,
    in_sem, fy_sem, core_sem, y_sem, z_sem, x_sem, red_sem,
):
    slabs, per, rows = acc.shape[0], acc.shape[1], acc.shape[4]
    nx = fx_ref.shape[0]
    ny_loc = fy_ref.shape[0]
    ra, rb = fx_ref.shape[1], fy_ref.shape[1]
    half_a = ra // N_CORE
    nz = field.shape[3]
    at = lax.axis_index("gy")
    var = lax.axis_index("var")
    core = at % N_CORE
    y = (at // N_CORE) % n_y
    z = at // (N_CORE * n_y)

    def device(pz=z, py=y, pc=core, pv=var):
        return ((pz * n_y + py) * N_CORE + pc, pv)

    sibling = device(pc=1 - core)
    axes = [
        (N_CORE, core, lambda k: device(pc=k)),
        (n_var, var, lambda k: device(pv=k)),
        (n_y, y, lambda k: device(py=k)),
        (N_Z, z, lambda k: device(pz=k)),
    ]

    loads = [
        pltpu.make_async_copy(field.at[pl.ds(s * per, per)], fbuf.at[s], in_sem.at[s])
        for s in range(slabs)
    ]
    for load in loads:
        load.start()

    barrier = pltpu.get_barrier_semaphore()
    others = 0
    for n, me, who in axes:
        for d in range(1, n):
            pl.semaphore_signal(
                barrier, inc=1, device_id=who(lax.rem(me + d, n)), device_id_type=MESH)
            others += 1

    w_x = split(kron_eye(fx_ref[...], 8))
    fy_own[...] = jnp.zeros_like(fy_own)
    fy_own[:, :rb] = fy_ref[...]
    pl.semaphore_wait(barrier, others)

    def remote(src, dst, sems, index, where):
        return pltpu.make_async_remote_copy(
            src_ref=src, dst_ref=dst,
            send_sem=sems.at[(0,) + index], recv_sem=sems.at[(1,) + index],
            device_id=where, device_id_type=MESH)

    fy_copy = remote(fy_own, fy_sib, fy_sem, (0,), sibling)
    fy_copy.start()

    def core_copy(s):
        return remote(ax.at[1 - core, s], axr.at[s], core_sem, (s,), sibling)

    for s in range(slabs):
        loads[s].wait()
        for g in range(0, ny_loc, 8):
            block = jnp.concatenate(
                [fbuf[s, v, :, g:g + 8, :].reshape(nx * 8, nz) for v in range(per)], axis=1)
            out = three(w_x, split(block))
            for h in range(N_CORE):
                for v in range(per):
                    piece = out[h * half_a * 8:(h + 1) * half_a * 8, v * nz:(v + 1) * nz]
                    ax[h, s, v, :, g:g + 8, :] = piece.reshape(half_a, 8, nz)
        core_copy(s).start()

    w_own = split(eye_kron(fy_own[:, :rb], half_a))
    fy_copy.wait()
    w_sib = split(eye_kron(fy_sib[:, :rb], half_a))

    def line(s, hop, n, pos, view, right, left, sems, who):
        @pl.when(pos == hop)
        def _():
            for j in range(n - 1, hop - 1, -1):
                if hop > 0:
                    remote(view(acc, s, j), view(right, s, j), sems, (0, s, j), who(hop - 1)).wait_recv()
                    view(acc, s, j)[...] += view(right, s, j)[...]
                if j > hop:
                    remote(view(acc, s, j), view(right, s, j), sems, (0, s, j), who(hop + 1)).start()
        mine = n - 1 - hop

        @pl.when(pos == mine)
        def _():
            for j in range(0, mine + 1):
                if hop > 0:
                    remote(view(acc, s, j), view(left, s, j), sems, (1, s, j), who(mine + 1)).wait_recv()
                    view(acc, s, j)[...] += view(left, s, j)[...]
                if j < mine:
                    remote(view(acc, s, j), view(left, s, j), sems, (1, s, j), who(mine - 1)).start()

    def line_end(n, pos, view, right, left, sems, who):
        for p in range(n):
            @pl.when(pos == p)
            def _():
                for s in range(slabs):
                    for j in range(p + 1, n):
                        remote(view(acc, s, j), view(right, s, j), sems, (0, s, j), who(p + 1)).wait_send()
                    for j in range(p):
                        remote(view(acc, s, j), view(left, s, j), sems, (1, s, j), who(p - 1)).wait_send()

    def view_y(ref, s, j):
        return ref.at[s, :, j]

    def view_z(ref, s, j):
        if ref is acc:
            return ref.at[s, :, y, j]
        return ref.at[s, :, j]

    y_args = (n_y, y, view_y, y_right, y_left, y_sem, axes[2][2])
    z_args = (N_Z, z, view_z, z_right, z_left, z_sem, axes[3][2])
    part = rows // n_var

    def x_copy(s, to, slot, src_var):
        return remote(acc.at[s, :, y, z, pl.ds(pl.multiple_of(to * part, part), part)],
                      pown.at[src_var, s], x_sem, (s, slot), device(pv=to))

    for t in range(slabs + n_y - 1 + N_Z - 1):
        if t < slabs:
            core_copy(t).wait_recv()
            own = jnp.concatenate(
                [ax[core, t, v].reshape(half_a * ny_loc, nz) for v in range(per)], axis=1)
            sib = jnp.concatenate(
                [axr[t, v].reshape(half_a * ny_loc, nz) for v in range(per)], axis=1)
            out = three(w_own, split(own)) + three(w_sib, split(sib))
            for v in range(per):
                acc[t, v] = out[:, v * nz:(v + 1) * nz].reshape(n_y, N_Z, rows, nz)
        for hop in range(n_y):
            if 0 <= t - hop < slabs:
                line(t - hop, hop, *y_args)
        for hop in range(N_Z):
            s = t - (n_y - 1) - hop
            if 0 <= s < slabs:
                line(s, hop, *z_args)
                if hop == N_Z - 1:
                    for d in range(1, n_var):
                        x_copy(s, lax.rem(var + d, n_var), d, var).start()
                    keep = pl.ds(pl.multiple_of(var * part, part), part)
                    pown[var, s] = acc[s, :, y, z, keep, :]

    w_v = kron_eye(fv_ref[...], 8)
    for s in range(slabs):
        for d in range(1, n_var):
            x_copy(s, lax.rem(var + d, n_var), d, lax.rem(var + n_var - d, n_var)).wait()

    def octet(o):
        return pown[:, :, :, o:o + 8, :].reshape(n_var * slabs * per * 8, nz)

    gram_z = jnp.zeros((nz, nz), F32)
    for o in range(0, part, 8):
        wide = exact(w_v, octet(o))
        gram_z += exact(wide.T, wide)
    raw = exact(gram_z, fz_ref[...])

    def total(value, buf, base):
        first = 0
        for n, me, who in axes:
            buf[first + me] = value
            copies = []
            for d in range(1, n):
                copies.append(remote(
                    buf.at[first + me], buf.at[first + me], red_sem,
                    (base + first + d,), who(lax.rem(me + d, n))))
                copies[-1].start()
            for copy in copies:
                copy.wait()
            value = buf[first]
            for k in range(1, n):
                value = value + buf[first + k]
            first += n
        return value

    slots = sum(n for n, _, _ in axes)
    half = nz // 2
    packed = total(jnp.concatenate([raw[:half], raw[half:]], axis=1), red_z, 0)
    width = raw.shape[1]
    raw = jnp.concatenate([packed[:, :width], packed[:, width:]], axis=0)
    basis_t = orth_rows(raw.T)
    proj_z_ref[...] = exact(basis_t.T, basis_t)

    nv = n_var * slabs * per
    cross = jnp.zeros((nv * 8, nv * 8), F32)
    for o in range(0, part, 8):
        wide = exact(octet(o), basis_t, 1, 1)
        cross += exact(wide, wide, 1, 1)
    cross = cross * spread((nv * 8, nv * 8), 1, 8, 1, 8)
    fold = exact(spread((nv, nv * 8), 1, nv, 8, nv), cross)
    gram_v = exact(fold, spread((nv * 8, 128), 8, nv, 1, 128))
    gram_v = total(gram_v, red_v, slots)[:, :nv]
    new_t = orth_rows(exact(gram_v, fv_ref[...]).T)
    proj_v_ref[...] = exact(new_t.T, new_t)
    energy = exact(new_t, gram_v) * new_t
    rms_ref[...] = jnp.sqrt(
        jnp.sum(jnp.sum(energy, axis=1, keepdims=True), axis=0, keepdims=True) * (1.0 / core_size))

    for s in range(slabs):
        core_copy(s).wait_send()
    line_end(*y_args)
    line_end(*z_args)


def per_device(n_gy, n_var, field, fx, fy, fz, fv):
    n_y = n_gy // (N_Z * N_CORE)
    v_loc, nx, ny_loc, nz = field.shape
    per = 2
    slabs = v_loc // per
    ra, rb = fx.shape[1], fy.shape[1]
    half_a = ra // N_CORE
    rows = half_a * rb // (n_y * N_Z)
    part = rows // n_var
    nv = fv.shape[0]
    slots = N_CORE + n_var + n_y + N_Z
    core_size = fv.shape[1] * ra * rb * fz.shape[1]
    vmem = pl.BlockSpec(memory_space=pltpu.VMEM)
    big = (slabs, per, n_y, N_Z, rows, nz)
    small = (slabs, per, N_Z, rows, nz)
    dma = pltpu.SemaphoreType.DMA
    proj_z, proj_v, rms = pl.pallas_call(
        functools.partial(kernel, n_y, n_var, core_size),
        out_shape=(
            jax.ShapeDtypeStruct((nz, nz), F32),
            jax.ShapeDtypeStruct((nv, nv), F32),
            jax.ShapeDtypeStruct((1, 1), F32),
        ),
        in_specs=[pl.BlockSpec(memory_space=pl.ANY), vmem, vmem, vmem, vmem],
        out_specs=(vmem, vmem, vmem),
        scratch_shapes=[
            pltpu.VMEM((slabs, per, nx, ny_loc, nz), F32),
            pltpu.VMEM((N_CORE, slabs, per, half_a, ny_loc, nz), F32),
            pltpu.VMEM((slabs, per, half_a, ny_loc, nz), F32),
            pltpu.VMEM((ny_loc, 128), F32),
            pltpu.VMEM((ny_loc, 128), F32),
            pltpu.VMEM(big, F32),
            pltpu.VMEM(big, F32),
            pltpu.VMEM(big, F32),
            pltpu.VMEM(small, F32),
            pltpu.VMEM(small, F32),
            pltpu.VMEM((n_var, slabs, per, part, nz), F32),
            pltpu.VMEM((slots, nz // 2, 2 * fz.shape[1]), F32),
            pltpu.VMEM((slots, nv, 128), F32),
            dma((slabs,)),
            dma((2, 1)),
            dma((2, slabs)),
            dma((2, 2, slabs, n_y)),
            dma((2, 2, slabs, N_Z)),
            dma((2, slabs, n_var)),
            dma((2, 2 * slots)),
        ],
        compiler_params=pltpu.CompilerParams(
            collective_id=0, has_side_effects=True, vmem_limit_bytes=52 * 2**20),
        cost_estimate=pl.CostEstimate(
            flops=10**10, bytes_accessed=4 * v_loc * nx * ny_loc * nz, transcendentals=0),
    )(field, fx, fy, fz, fv)
    return proj_z, proj_v, rms[0, 0]


def solution(mesh):
    in_specs = (P("var", None, "gy", None), P(), P("gy", None), P(), P())
    return jax.shard_map(
        functools.partial(per_device, mesh.shape["gy"], mesh.shape["var"]),
        mesh=mesh, in_specs=in_specs, out_specs=(P(), P(), P()), check_vma=False,
    )
```

time: 1090 us -> 116 us (0.11)
  waiting for transfers between devices: 751 us -> 0 us
  matrix products: 185 us -> 0 us
  Pallas kernels: 0 us -> 109 us
  blocking collectives: 67.6 us -> 0 us
  local copies, waits for them, and re-layouts: 52 us -> 4.34 us
  other arithmetic: 16.1 us -> 0 us
  between operations: 16 us -> 2.42 us
    reduce_scatter x1 -> x0, waiting for transfers between devices: 360 us -> none  [per_device(): lax.psum_scatter(wide_z, ('gy', 'var'), scatter_dimension=3, tiled=True)]
    psum x2 -> x0, waiting for transfers between devices: 287 us -> none  [the longest x1 180 us: total_core(): return lax.psum(local_part, ('gy', 'var'))]
    dot_general x13 -> x0, matrix products: 185 us -> none  [the longest x1 109 us: per_device(): jnp.einsum('vabz,vc->cabz', partial_value, local_v, precision=precise)]
    pallas_call x0 -> x1, Pallas kernels: none -> 109 us  [per_device(): pl.pallas_call(functools.partial(kernel, n_y, n_var, core_size), out_shap...]
    all_gather x1 -> x0, waiting for transfers between devices: 103 us -> none  [per_device(): every_v = lax.all_gather(summed_v, 'var', axis=0, tiled=True)]
    all_gather x1 -> x0, blocking collectives: 67.6 us -> none  [per_device(): raw_z = lax.all_gather(rows_z, ('gy', 'var'), axis=0, tiled=True)]
    dot_general x3 -> x0, local copies, waits for them, and re-layouts: 42.8 us -> none  [the longest x1 42.7 us: per_device(): jnp.einsum('vabz,vc->cabz', partial_value, local_v, precision=precise)]
    another operation x10 -> x0, other arithmetic: 16.1 us -> none  [the longest x6 8.67 us: orth(): lower = jnp.linalg.cholesky(gram)]
  transfers between devices with their start and end apart: 4 -> 0, of which waited for: 4 -> 0; matrix products, arithmetic and copies ran while one was open for 0% -> 0% of each run, Pallas kernels for 0% -> 0%
where the time goes in v1:
time: 116 us; the launch traced here: 115 us
  Pallas kernels  109 us (94%)
  local copies, waits for them, and re-layouts  4.34 us (4%)
  between operations  2.42 us (2%)
    pallas_call x1, Pallas kernels, per_device(): pl.pallas_call(functools.partial(kernel, n_y, n_var, core_size), out_shap...  109 us
    unnamed x7, local copies, waits for them, and re-layouts  4.34 us

profile of v1, /device:TPU:0, one launch (start us, length us, event | category | flops | bytes accessed | tf_op | source)
XLA Modules:
  0.0 115.4 jit_solution(373927188547870889)
XLA Ops:
  0.6 0.8 copy.8.fx_ref
  1.4 0.8 copy.10.fv_ref
  2.2 0.8 copy.9.fz_ref
  3.0 0.0 copy-start
  3.0 0.7 copy-done
  3.7 108.6 %shard_map.76 = (f32[128,128]{1,0:T(8,128)S(1)}, f32[32,32]{1,0:T(8,128)S(1)}, f32[1,1]{1,0:T(1,128)}) custom-call(f32[16,32,32,128]{3,2,1,0:T(8,128)} %field.1, f32[32,16]{1,0:T(8,128)S(1)} %copy.8.fx_ref, f32[32,64]{1,0:T(8,128)S(1)} %copy-done, f32[128,64]{1,0:T(8,128)S(1)} %copy.9.fz_ref, f32[32,16]{1,0:T(8,128)S(1)} %copy.10.fv_ref), custom_call_target="tpu_custom_call" | custom-call | flops 10000000000 | bytes 8388608 | tf_op jit(solution)/shard_map/pallas_call | solution.py:307
  112.4 0.6 copy.14
  113.0 0.6 copy.15
Async XLA Ops:
  3.0 0.7 copy-start

commit v2 on v1

--- a/solution.py
+++ b/solution.py
@@ -26,9 +26,9 @@
     return high, (a - high.astype(F32)).astype(BF16)
 
 
-def three(a, b):
+def three(a, b, cb=0):
     def dot(p, q):
-        return lax.dot_general(p, q, (((1,), (0,)), ((), ())), preferred_element_type=F32)
+        return lax.dot_general(p, q, (((1,), (cb,)), ((), ())), preferred_element_type=F32)
     return dot(a[0], b[0]) + (dot(a[0], b[1]) + dot(a[1], b[0]))
 
 
@@ -42,9 +42,9 @@
     return (rows == cols).astype(F32)
 
 
-def kron_eye(factor, eye):
-    k, m = factor.shape
-    tall = exact(spread((m * eye, m), eye, m, 1, m), factor, 1, 1)
+def kron_eye(factor_t, eye):
+    m, k = factor_t.shape
+    tall = exact(spread((m * eye, m), eye, m, 1, m), factor_t)
     full = exact(tall, spread((k, k * eye), 1, k, eye, k))
     return full * spread((m * eye, k * eye), 1, eye, 1, eye)
 
@@ -80,17 +80,16 @@
 
 def kernel(
     n_y, n_var, core_size,
-    field, fx_ref, fy_ref, fz_ref, fv_ref,
+    field, fx_arg, fy_arg, fz_arg, fv_arg,
     proj_z_ref, proj_v_ref, rms_ref,
     fbuf, ax, axr, fy_own, fy_sib, acc,
-    y_right, y_left, z_right, z_left, pown,
-    red_z, red_v,
-    in_sem, fy_sem, core_sem, y_sem, z_sem, x_sem, red_sem,
+    early_right, early_left, late_right, late_left, pown,
+    red_z, red_v, fx_ref, fy_ref, fz_ref, fv_ref,
+    in_sem, arg_sem, fy_sem, core_sem, y_sem, z_sem, x_sem, red_sem,
 ):
     slabs, per, rows = acc.shape[0], acc.shape[1], acc.shape[4]
-    nx = fx_ref.shape[0]
-    ny_loc = fy_ref.shape[0]
-    ra, rb = fx_ref.shape[1], fy_ref.shape[1]
+    ra, nx = fx_ref.shape
+    ny_loc, rb = fy_ref.shape
     half_a = ra // N_CORE
     nz = field.shape[3]
     at = lax.axis_index("gy")
@@ -103,28 +102,35 @@
         return ((pz * n_y + py) * N_CORE + pc, pv)
 
     sibling = device(pc=1 - core)
-    axes = [
-        (N_CORE, core, lambda k: device(pc=k)),
-        (n_var, var, lambda k: device(pv=k)),
-        (n_y, y, lambda k: device(py=k)),
-        (N_Z, z, lambda k: device(pz=k)),
-    ]
+    pair = (N_CORE * n_var, var * N_CORE + core,
+            lambda k: device(pc=k % N_CORE, pv=k // N_CORE))
+    plane = (N_CORE * n_var * n_y, (y * n_var + var) * N_CORE + core,
+             lambda k: device(pc=k % N_CORE, pv=(k // N_CORE) % n_var, py=k // (N_CORE * n_var)))
+    along_y = (n_y, y, lambda k: device(py=k))
+    along_z = (N_Z, z, lambda k: device(pz=k))
 
     loads = [
         pltpu.make_async_copy(field.at[pl.ds(s * per, per)], fbuf.at[s], in_sem.at[s])
         for s in range(slabs)
     ]
-    for load in loads:
+    params = [
+        pltpu.make_async_copy(src, dst, arg_sem.at[i])
+        for i, (src, dst) in enumerate(
+            [(fx_arg, fx_ref), (fy_arg, fy_ref), (fz_arg, fz_ref), (fv_arg, fv_ref)])
+    ]
+    for load in params + loads:
         load.start()
 
     barrier = pltpu.get_barrier_semaphore()
     others = 0
-    for n, me, who in axes:
+    for n, me, who in (plane, along_z):
         for d in range(1, n):
             pl.semaphore_signal(
                 barrier, inc=1, device_id=who(lax.rem(me + d, n)), device_id_type=MESH)
             others += 1
 
+    for load in params:
+        load.wait()
     w_x = split(kron_eye(fx_ref[...], 8))
     fy_own[...] = jnp.zeros_like(fy_own)
     fy_own[:, :rb] = fy_ref[...]
@@ -142,7 +148,7 @@
     def core_copy(s):
         return remote(ax.at[1 - core, s], axr.at[s], core_sem, (s,), sibling)
 
-    for s in range(slabs):
+    def stage_x(s):
         loads[s].wait()
         for g in range(0, ny_loc, 8):
             block = jnp.concatenate(
@@ -154,10 +160,6 @@
                     ax[h, s, v, :, g:g + 8, :] = piece.reshape(half_a, 8, nz)
         core_copy(s).start()
 
-    w_own = split(eye_kron(fy_own[:, :rb], half_a))
-    fy_copy.wait()
-    w_sib = split(eye_kron(fy_sib[:, :rb], half_a))
-
     def line(s, hop, n, pos, view, right, left, sems, who):
         @pl.when(pos == hop)
         def _():
@@ -178,72 +180,97 @@
                 if j < mine:
                     remote(view(acc, s, j), view(left, s, j), sems, (1, s, j), who(mine - 1)).start()
 
-    def line_end(n, pos, view, right, left, sems, who):
+    def line_end(args_of):
+        n, pos = args_of(0)[:2]
         for p in range(n):
             @pl.when(pos == p)
             def _():
                 for s in range(slabs):
+                    _, _, view, right, left, sems, who = args_of(s)
                     for j in range(p + 1, n):
                         remote(view(acc, s, j), view(right, s, j), sems, (0, s, j), who(p + 1)).wait_send()
                     for j in range(p):
                         remote(view(acc, s, j), view(left, s, j), sems, (1, s, j), who(p - 1)).wait_send()
 
+    def z_first(s):
+        return s < slabs // 8
+
     def view_y(ref, s, j):
+        if ref is acc and z_first(s):
+            return ref.at[s, :, j, z]
         return ref.at[s, :, j]
 
     def view_z(ref, s, j):
-        if ref is acc:
-            return ref.at[s, :, y, j]
-        return ref.at[s, :, j]
-
-    y_args = (n_y, y, view_y, y_right, y_left, y_sem, axes[2][2])
-    z_args = (N_Z, z, view_z, z_right, z_left, z_sem, axes[3][2])
+        if not z_first(s):
+            return ref.at[s, :, y, j] if ref is acc else ref.at[s, :, j]
+        return ref.at[s, :, :, j]
+
+    def y_args(s):
+        bufs = (late_right, late_left) if z_first(s) else (early_right, early_left)
+        return (n_y, y, view_y) + bufs + (y_sem, along_y[2])
+
+    def z_args(s):
+        bufs = (early_right, early_left) if z_first(s) else (late_right, late_left)
+        return (N_Z, z, view_z) + bufs + (z_sem, along_z[2])
     part = rows // n_var
 
     def x_copy(s, to, slot, src_var):
         return remote(acc.at[s, :, y, z, pl.ds(pl.multiple_of(to * part, part), part)],
                       pown.at[src_var, s], x_sem, (s, slot), device(pv=to))
 
-    for t in range(slabs + n_y - 1 + N_Z - 1):
+    def stage_y(s):
+        core_copy(s).wait_recv()
+        own = jnp.concatenate(
+            [ax[core, s, v].reshape(half_a * ny_loc, nz) for v in range(per)], axis=1)
+        sib = jnp.concatenate(
+            [axr[s, v].reshape(half_a * ny_loc, nz) for v in range(per)], axis=1)
+        out = three(w_own, split(own)) + three(w_sib, split(sib))
+        for v in range(per):
+            acc[s, v] = out[:, v * nz:(v + 1) * nz].reshape(n_y, N_Z, rows, nz)
+
+    ahead = 2
+    for s in range(ahead):
+        stage_x(s)
+    w_own = split(eye_kron(fy_own[:, :rb], half_a))
+    fy_copy.wait()
+    w_sib = split(eye_kron(fy_sib[:, :rb], half_a))
+    for t in range(slabs + n_y + N_Z):
+        if t + ahead < slabs:
+            stage_x(t + ahead)
         if t < slabs:
-            core_copy(t).wait_recv()
-            own = jnp.concatenate(
-                [ax[core, t, v].reshape(half_a * ny_loc, nz) for v in range(per)], axis=1)
-            sib = jnp.concatenate(
-                [axr[t, v].reshape(half_a * ny_loc, nz) for v in range(per)], axis=1)
-            out = three(w_own, split(own)) + three(w_sib, split(sib))
-            for v in range(per):
-                acc[t, v] = out[:, v * nz:(v + 1) * nz].reshape(n_y, N_Z, rows, nz)
-        for hop in range(n_y):
-            if 0 <= t - hop < slabs:
-                line(t - hop, hop, *y_args)
-        for hop in range(N_Z):
-            s = t - (n_y - 1) - hop
-            if 0 <= s < slabs:
-                line(s, hop, *z_args)
-                if hop == N_Z - 1:
-                    for d in range(1, n_var):
-                        x_copy(s, lax.rem(var + d, n_var), d, var).start()
-                    keep = pl.ds(pl.multiple_of(var * part, part), part)
-                    pown[var, s] = acc[s, :, y, z, keep, :]
-
-    w_v = kron_eye(fv_ref[...], 8)
+            stage_y(t)
+        if t == slabs - 1:
+            w_v = split(kron_eye(fv_ref[...], 8))
+        for s in range(min(t, slabs - 1), -1, -1):
+            lag = t - s
+            stages = [z_args(s), y_args(s)] if z_first(s) else [y_args(s), z_args(s)]
+            n_first, n_second = stages[0][0], stages[1][0]
+            if lag == 0:
+                line(s, 0, *stages[0])
+            if 2 <= lag <= n_first:
+                line(s, lag - 1, *stages[0])
+            if n_first <= lag < n_first + n_second:
+                line(s, lag - n_first, *stages[1])
+            if lag == n_first + n_second - 1:
+                for d in range(1, n_var):
+                    x_copy(s, lax.rem(var + d, n_var), d, var).start()
+                keep = pl.ds(pl.multiple_of(var * part, part), part)
+                pown[var, s] = acc[s, :, y, z, keep, :]
+
     for s in range(slabs):
         for d in range(1, n_var):
             x_copy(s, lax.rem(var + d, n_var), d, lax.rem(var + n_var - d, n_var)).wait()
 
-    def octet(o):
-        return pown[:, :, :, o:o + 8, :].reshape(n_var * slabs * per * 8, nz)
-
-    gram_z = jnp.zeros((nz, nz), F32)
-    for o in range(0, part, 8):
-        wide = exact(w_v, octet(o))
-        gram_z += exact(wide.T, wide)
-    raw = exact(gram_z, fz_ref[...])
-
-    def total(value, buf, base):
+    nv = n_var * slabs * per
+    octets = [pown[:, :, :, o:o + 8, :].reshape(nv * 8, nz) for o in range(0, part, 8)]
+    wide = three(w_v, split(jnp.concatenate(octets, axis=1)))
+    wide = jnp.concatenate(
+        [wide[:, k * nz:(k + 1) * nz] for k in range(len(octets))], axis=0)
+    raw = exact(three(split(wide.T), split(wide)), fz_ref[...], 1, 1)
+
+    def total(value, groups, buf, base):
         first = 0
-        for n, me, who in axes:
+        for n, me, who in groups:
             buf[first + me] = value
             copies = []
             for d in range(1, n):
@@ -259,24 +286,26 @@
             first += n
         return value
 
-    slots = sum(n for n, _, _ in axes)
     half = nz // 2
-    packed = total(jnp.concatenate([raw[:half], raw[half:]], axis=1), red_z, 0)
+    packed = total(
+        jnp.concatenate([raw[:half], raw[half:]], axis=1), (pair, along_y, along_z), red_z, 0)
     width = raw.shape[1]
     raw = jnp.concatenate([packed[:, :width], packed[:, width:]], axis=0)
     basis_t = orth_rows(raw.T)
-    proj_z_ref[...] = exact(basis_t.T, basis_t)
-
-    nv = n_var * slabs * per
-    cross = jnp.zeros((nv * 8, nv * 8), F32)
-    for o in range(0, part, 8):
-        wide = exact(octet(o), basis_t, 1, 1)
-        cross += exact(wide, wide, 1, 1)
+
+    tall = three(split(jnp.concatenate(octets, axis=0)), split(basis_t), 1)
+    wide = split(jnp.concatenate(
+        [tall[k * nv * 8:(k + 1) * nv * 8] for k in range(len(octets))], axis=1))
+    cross = three(wide, wide, 1)
     cross = cross * spread((nv * 8, nv * 8), 1, 8, 1, 8)
     fold = exact(spread((nv, nv * 8), 1, nv, 8, nv), cross)
-    gram_v = exact(fold, spread((nv * 8, 128), 8, nv, 1, 128))
-    gram_v = total(gram_v, red_v, slots)[:, :nv]
-    new_t = orth_rows(exact(gram_v, fv_ref[...]).T)
+    gram_v = exact(fold, spread((nv * 8, nv), 8, nv, 1, nv))
+    packed = total(
+        jnp.concatenate([gram_v[k:k + 8] for k in range(0, nv, 8)], axis=1),
+        (plane, along_z), red_v, red_z.shape[0])
+    gram_v = jnp.concatenate([packed[:, k * nv:(k + 1) * nv] for k in range(nv // 8)], axis=0)
+    proj_z_ref[...] = exact(basis_t.T, basis_t)
+    new_t = orth_rows(exact(fv_ref[...], gram_v))
     proj_v_ref[...] = exact(new_t.T, new_t)
     energy = exact(new_t, gram_v) * new_t
     rms_ref[...] = jnp.sqrt(
@@ -284,21 +313,22 @@
 
     for s in range(slabs):
         core_copy(s).wait_send()
-    line_end(*y_args)
-    line_end(*z_args)
+    line_end(y_args)
+    line_end(z_args)
 
 
 def per_device(n_gy, n_var, field, fx, fy, fz, fv):
     n_y = n_gy // (N_Z * N_CORE)
     v_loc, nx, ny_loc, nz = field.shape
-    per = 2
+    per = 1
     slabs = v_loc // per
     ra, rb = fx.shape[1], fy.shape[1]
     half_a = ra // N_CORE
     rows = half_a * rb // (n_y * N_Z)
     part = rows // n_var
     nv = fv.shape[0]
-    slots = N_CORE + n_var + n_y + N_Z
+    slots_z = N_CORE * n_var + n_y + N_Z
+    slots_v = N_CORE * n_var * n_y + N_Z
     core_size = fv.shape[1] * ra * rb * fz.shape[1]
     vmem = pl.BlockSpec(memory_space=pltpu.VMEM)
     big = (slabs, per, n_y, N_Z, rows, nz)
@@ -311,7 +341,7 @@
             jax.ShapeDtypeStruct((nv, nv), F32),
             jax.ShapeDtypeStruct((1, 1), F32),
         ),
-        in_specs=[pl.BlockSpec(memory_space=pl.ANY), vmem, vmem, vmem, vmem],
+        in_specs=[pl.BlockSpec(memory_space=pl.ANY)] * 5,
         out_specs=(vmem, vmem, vmem),
         scratch_shapes=[
             pltpu.VMEM((slabs, per, nx, ny_loc, nz), F32),
@@ -325,21 +355,26 @@
             pltpu.VMEM(small, F32),
             pltpu.VMEM(small, F32),
             pltpu.VMEM((n_var, slabs, per, part, nz), F32),
-            pltpu.VMEM((slots, nz // 2, 2 * fz.shape[1]), F32),
-            pltpu.VMEM((slots, nv, 128), F32),
+            pltpu.VMEM((slots_z, nz // 2, 2 * fz.shape[1]), F32),
+            pltpu.VMEM((slots_v, 8, nv * nv // 8), F32),
+            pltpu.VMEM(fx.shape[::-1], F32),
+            pltpu.VMEM(fy.shape, F32),
+            pltpu.VMEM(fz.shape[::-1], F32),
+            pltpu.VMEM(fv.shape[::-1], F32),
             dma((slabs,)),
+            dma((4,)),
             dma((2, 1)),
             dma((2, slabs)),
             dma((2, 2, slabs, n_y)),
             dma((2, 2, slabs, N_Z)),
             dma((2, slabs, n_var)),
-            dma((2, 2 * slots)),
+            dma((2, slots_z + slots_v)),
         ],
         compiler_params=pltpu.CompilerParams(
             collective_id=0, has_side_effects=True, vmem_limit_bytes=52 * 2**20),
         cost_estimate=pl.CostEstimate(
             flops=10**10, bytes_accessed=4 * v_loc * nx * ny_loc * nz, transcendentals=0),
-    )(field, fx, fy, fz, fv)
+    )(field, fx.T, fy, fz.T, fv.T)
     return proj_z, proj_v, rms[0, 0]
 
 

time: 116 us -> 112 us (0.966)
  Pallas kernels: 109 us -> 105 us
    pallas_call x1, Pallas kernels: 109 us -> 105 us  [per_device(): pl.pallas_call(functools.partial(kernel, n_y, n_var, core_size), out_shap...]
    unnamed x7 -> x10, local copies, waits for them, and re-layouts: 4.34 us -> 4.1 us
where the time goes in v2:
time: 112 us; the launch traced here: 111 us
  Pallas kernels  105 us (94%)
  local copies, waits for them, and re-layouts  4.1 us (4%)
  between operations  2.4 us (2%)
    pallas_call x1, Pallas kernels, per_device(): pl.pallas_call(functools.partial(kernel, n_y, n_var, core_size), out_shap...  105 us
    unnamed x10, local copies, waits for them, and re-layouts  4.1 us

profile of v2, /device:TPU:0, one launch (start us, length us, event | category | flops | bytes accessed | tf_op | source)
XLA Modules:
  0.0 111.3 jit_solution(7129912050592205195)
XLA Ops:
  0.6 0.0 copy-start
  0.6 0.7 copy-done
  1.4 0.0 copy-start.1
  1.4 0.7 copy-done.1
  2.1 0.0 copy-start.2
  2.1 0.7 copy-done.2
  2.8 0.0 copy-start.3
  2.8 0.7 copy-done.3
  3.5 104.8 %shard_map.76 = (f32[128,128]{1,0:T(8,128)S(1)}, f32[32,32]{1,0:T(8,128)S(1)}, f32[1,1]{1,0:T(1,128)}) custom-call(f32[16,32,32,128]{3,2,1,0:T(8,128)} %field.1, f32[16,32]{1,0:T(8,128)S(1)} %bitcast.5, f32[32,64]{1,0:T(8,128)S(1)} %copy-done.1, f32[64,128]{1,0:T(8,128)S(1)} %bitcast.4, f32[16,32]{1,0:T(8,128)S(1)} %bitcast.6), custom_call_target="tpu_custom_call" | custom-call | flops 10000000000 | bytes 8388608 | tf_op jit(solution)/shard_map/pallas_call | solution.py:337
  108.3 0.6 copy.11
  108.9 0.6 copy.12
Async XLA Ops:
  0.6 0.8 copy-start
  1.4 0.7 copy-start.1
  2.1 0.7 copy-start.2
  2.8 0.7 copy-start.3

commit v3 on v2

--- a/solution.py
+++ b/solution.py
@@ -78,6 +78,13 @@
     return jnp.concatenate(done, axis=0)
 
 
+def each(count, body, first=0):
+    def step(t, carry):
+        body(t)
+        return carry
+    lax.fori_loop(first, count, step, 0)
+
+
 def kernel(
     n_y, n_var, core_size,
     field, fx_arg, fy_arg, fz_arg, fv_arg,
@@ -109,17 +116,17 @@
     along_y = (n_y, y, lambda k: device(py=k))
     along_z = (N_Z, z, lambda k: device(pz=k))
 
-    loads = [
-        pltpu.make_async_copy(field.at[pl.ds(s * per, per)], fbuf.at[s], in_sem.at[s])
-        for s in range(slabs)
-    ]
+    def load_of(s):
+        return pltpu.make_async_copy(field.at[pl.ds(s * per, per)], fbuf.at[s], in_sem.at[s])
+
     params = [
         pltpu.make_async_copy(src, dst, arg_sem.at[i])
         for i, (src, dst) in enumerate(
             [(fx_arg, fx_ref), (fy_arg, fy_ref), (fz_arg, fz_ref), (fv_arg, fv_ref)])
     ]
-    for load in params + loads:
+    for load in params:
         load.start()
+    each(slabs, lambda s: load_of(s).start())
 
     barrier = pltpu.get_barrier_semaphore()
     others = 0
@@ -149,7 +156,7 @@
         return remote(ax.at[1 - core, s], axr.at[s], core_sem, (s,), sibling)
 
     def stage_x(s):
-        loads[s].wait()
+        load_of(s).wait()
         for g in range(0, ny_loc, 8):
             block = jnp.concatenate(
                 [fbuf[s, v, :, g:g + 8, :].reshape(nx * 8, nz) for v in range(per)], axis=1)
@@ -180,38 +187,25 @@
                 if j < mine:
                     remote(view(acc, s, j), view(left, s, j), sems, (1, s, j), who(mine - 1)).start()
 
-    def line_end(args_of):
-        n, pos = args_of(0)[:2]
+    def line_end(n, pos, view, right, left, sems, who):
         for p in range(n):
             @pl.when(pos == p)
             def _():
-                for s in range(slabs):
-                    _, _, view, right, left, sems, who = args_of(s)
+                def ends(s):
                     for j in range(p + 1, n):
                         remote(view(acc, s, j), view(right, s, j), sems, (0, s, j), who(p + 1)).wait_send()
                     for j in range(p):
                         remote(view(acc, s, j), view(left, s, j), sems, (1, s, j), who(p - 1)).wait_send()
-
-    def z_first(s):
-        return s < slabs // 8
+                each(slabs, ends)
 
     def view_y(ref, s, j):
-        if ref is acc and z_first(s):
-            return ref.at[s, :, j, z]
         return ref.at[s, :, j]
 
     def view_z(ref, s, j):
-        if not z_first(s):
-            return ref.at[s, :, y, j] if ref is acc else ref.at[s, :, j]
-        return ref.at[s, :, :, j]
-
-    def y_args(s):
-        bufs = (late_right, late_left) if z_first(s) else (early_right, early_left)
-        return (n_y, y, view_y) + bufs + (y_sem, along_y[2])
-
-    def z_args(s):
-        bufs = (early_right, early_left) if z_first(s) else (late_right, late_left)
-        return (N_Z, z, view_z) + bufs + (z_sem, along_z[2])
+        return ref.at[s, :, y, j] if ref is acc else ref.at[s, :, j]
+
+    y_args = (n_y, y, view_y, early_right, early_left, y_sem, along_y[2])
+    z_args = (N_Z, z, view_z, late_right, late_left, z_sem, along_z[2])
     part = rows // n_var
 
     def x_copy(s, to, slot, src_var):
@@ -229,37 +223,44 @@
             acc[s, v] = out[:, v * nz:(v + 1) * nz].reshape(n_y, N_Z, rows, nz)
 
     ahead = 2
-    for s in range(ahead):
-        stage_x(s)
+    each(ahead, stage_x)
     w_own = split(eye_kron(fy_own[:, :rb], half_a))
     fy_copy.wait()
     w_sib = split(eye_kron(fy_sib[:, :rb], half_a))
-    for t in range(slabs + n_y + N_Z):
-        if t + ahead < slabs:
+    w_v = split(kron_eye(fv_ref[...], 8))
+
+    def x_send(s):
+        for d in range(1, n_var):
+            x_copy(s, lax.rem(var + d, n_var), d, var).start()
+        keep = pl.ds(pl.multiple_of(var * part, part), part)
+        pown[var, s] = acc[s, :, y, z, keep, :]
+
+    plan = [(0, lambda s: line(s, 0, *y_args))]
+    plan += [(h + 1, lambda s, h=h: line(s, h, *y_args)) for h in range(1, n_y)]
+    plan += [(n_y + h, lambda s, h=h: line(s, h, *z_args)) for h in range(N_Z)]
+    plan += [(n_y + N_Z - 1, x_send)]
+
+    def step(t):
+        @pl.when(t + ahead < slabs)
+        def _():
             stage_x(t + ahead)
-        if t < slabs:
+
+        @pl.when(t < slabs)
+        def _():
             stage_y(t)
-        if t == slabs - 1:
-            w_v = split(kron_eye(fv_ref[...], 8))
-        for s in range(min(t, slabs - 1), -1, -1):
-            lag = t - s
-            stages = [z_args(s), y_args(s)] if z_first(s) else [y_args(s), z_args(s)]
-            n_first, n_second = stages[0][0], stages[1][0]
-            if lag == 0:
-                line(s, 0, *stages[0])
-            if 2 <= lag <= n_first:
-                line(s, lag - 1, *stages[0])
-            if n_first <= lag < n_first + n_second:
-                line(s, lag - n_first, *stages[1])
-            if lag == n_first + n_second - 1:
-                for d in range(1, n_var):
-                    x_copy(s, lax.rem(var + d, n_var), d, var).start()
-                keep = pl.ds(pl.multiple_of(var * part, part), part)
-                pown[var, s] = acc[s, :, y, z, keep, :]
-
-    for s in range(slabs):
+
+        for lag, act in plan:
+            @pl.when((t >= lag) & (t - lag < slabs))
+            def _(lag=lag, act=act):
+                act(t - lag)
+
+    each(slabs + n_y + N_Z - 1, step)
+
+    def x_wait(s):
         for d in range(1, n_var):
             x_copy(s, lax.rem(var + d, n_var), d, lax.rem(var + n_var - d, n_var)).wait()
+
+    each(slabs, x_wait)
 
     nv = n_var * slabs * per
     octets = [pown[:, :, :, o:o + 8, :].reshape(nv * 8, nz) for o in range(0, part, 8)]
@@ -311,10 +312,9 @@
     rms_ref[...] = jnp.sqrt(
         jnp.sum(jnp.sum(energy, axis=1, keepdims=True), axis=0, keepdims=True) * (1.0 / core_size))
 
-    for s in range(slabs):
-        core_copy(s).wait_send()
-    line_end(y_args)
-    line_end(z_args)
+    each(slabs, lambda s: core_copy(s).wait_send())
+    line_end(*y_args)
+    line_end(*z_args)
 
 
 def per_device(n_gy, n_var, field, fx, fy, fz, fv):

time: 112 us -> 108 us (0.964)
  Pallas kernels: 105 us -> 101 us
    pallas_call x1, Pallas kernels: 105 us -> 101 us  [per_device(): pl.pallas_call(functools.partial(kernel, n_y, n_var, core_size), out_shap...]
where the time goes in v3:
time: 108 us; the launch traced here: 107 us
  Pallas kernels  101 us (94%)
  local copies, waits for them, and re-layouts  4.1 us (4%)
  between operations  2.4 us (2%)
    pallas_call x1, Pallas kernels, per_device(): pl.pallas_call(functools.partial(kernel, n_y, n_var, core_size), out_shap...  101 us
    unnamed x10, local copies, waits for them, and re-layouts  4.1 us

profile of v3, /device:TPU:0, one launch (start us, length us, event | category | flops | bytes accessed | tf_op | source)
XLA Modules:
  0.0 107.3 jit_solution(16817519249849870394)
XLA Ops:
  0.6 0.0 copy-start
  0.6 0.7 copy-done
  1.4 0.0 copy-start.1
  1.4 0.7 copy-done.1
  2.1 0.0 copy-start.2
  2.1 0.7 copy-done.2
  2.8 0.0 copy-start.3
  2.8 0.7 copy-done.3
  3.5 100.8 %shard_map.76 = (f32[128,128]{1,0:T(8,128)S(1)}, f32[32,32]{1,0:T(8,128)S(1)}, f32[1,1]{1,0:T(1,128)}) custom-call(f32[16,32,32,128]{3,2,1,0:T(8,128)} %field.1, f32[16,32]{1,0:T(8,128)S(1)} %bitcast.5, f32[32,64]{1,0:T(8,128)S(1)} %copy-done.1, f32[64,128]{1,0:T(8,128)S(1)} %bitcast.4, f32[16,32]{1,0:T(8,128)S(1)} %bitcast.6), custom_call_target="tpu_custom_call" | custom-call | flops 10000000000 | bytes 8388608 | tf_op jit(solution)/shard_map/pallas_call | solution.py:337
  104.4 0.6 copy.11
  105.0 0.6 copy.12
Async XLA Ops:
  0.6 0.8 copy-start
  1.4 0.7 copy-start.1
  2.1 0.7 copy-start.2
  2.8 0.7 copy-start.3
